TPU v7x, 32 devices: a whole 2x2x4 slice. The times are simulated.
32 devices in a mesh: row: 4 (over y, core), col: 8 (over z, x).
Axes of the slice: x: 2, y: 2, z: 4, core: 2. Of those that a mesh axis runs over, the one named last changes fastest.
Arguments:
- inverse_slab: bfloat16 [65536, 2048], P('row', 'col'), may hold values from -0.0234375 to 0.0234375
- cot_solved: bfloat16 [64, 65536], P(None, ('row', 'col')), may hold values from -6 to 6
- cot_direct: bfloat16 [64, 2048], P(None, 'col'), may hold values from -6 to 6
- solved_panel: bfloat16 [64, 65536], P(None, 'col'), may hold values from -1.078125 to 1.078125
Outputs:
- grad_factor: float32 [64, 2048], P(None, 'col')
- grad_operator: bfloat16 [2048, 65536], P('row', 'col')
All inputs are finite; a program needn't handle non-finite values.
Results may differ from a plain program's by a relative error of at most 0.0049.
Values may be sent and summed in bfloat16 or wider, within the bound.
A program may use at most 64 MiB of HBM per device.

v0:
```python
import jax
import jax.numpy as jnp
from jax import lax
from jax.sharding import PartitionSpec as P


def body(inverse_slab, cot_solved, cot_direct, solved_panel):
    scale = 1.0 / jnp.sqrt(jnp.float32(2.0))
    block_rows = lax.all_gather(cot_solved, "col", axis=1, tiled=True)
    partial_sum = jnp.dot(block_rows, inverse_slab, preferred_element_type=jnp.float32)
    pulled = lax.psum(partial_sum, "row")
    grad_factor = (cot_direct.astype(jnp.float32) + pulled) * scale
    pulled_low = pulled.astype(jnp.bfloat16)
    width = pulled_low.shape[1]
    factor = lax.axis_size("col") // lax.axis_size("row")
    gathered = lax.all_gather(pulled_low, "col", axis=1, tiled=True)
    offset = lax.axis_index("row") * (factor * width)
    needed = lax.dynamic_slice_in_dim(gathered, offset, factor * width, 1)
    product = lax.dot_general(
        needed, solved_panel, (((0,), (0,)), ((), ())), preferred_element_type=jnp.float32
    )
    grad_operator = (product * -scale).astype(jnp.bfloat16)
    return (grad_factor, grad_operator)


def solution(mesh):
    in_specs = (P("row", "col"), P(None, ("row", "col")), P(None, "col"), P(None, "col"))
    out_specs = (P(None, "col"), P("row", "col"))
    return jax.shard_map(body, mesh=mesh, in_specs=in_specs, out_specs=out_specs, check_vma=False)
```

profile of v0, /device:TPU:0, one launch (start us, length us, event | category | flops | bytes accessed | tf_op | source)
XLA Modules:
  0.0 143.1 jit_solution(4705360385696968003)
XLA Ops:
  7.2 0.0 copy-start
  7.2 0.0 all-gather.2.cloned.1.call-start
  7.2 0.7 all-gather.2.cloned.1.call-update
  7.9 0.0 copy-start.1
  7.9 0.0 all-reduce.2.cloned.1.call-start
  8.0 54.2 %all-gather.2.cloned.1.call-done = bf16[64,16384]{1,0:T(8,128)(2,1)} async-done(((bf16[64,2048]{1,0:T(8,128)(2,1)}), bf16[64,16384]{1,0:T(8,128)(2,1)}) %all-gather.2.cloned.1.call-update) | async-done | bytes 2097168 | tf_op jit(solution)/shard_map/all_gather | solution.py:9
  62.2 6.1 %fusion.3 = f32[64,256]{1,0:T(8,128)} fusion(bf16[64,16384]{1,0:T(8,128)(2,1)} %all-gather.2.cloned.1.call-done, bf16[16384,256]{1,0:T(8,128)(2,1)} %param.4), kind=kOutput, calls=%fused_computation.5 | convolution fusion | flops 536870912 | bytes 10551296 | tf_op jit(solution)/shard_map/dot_general | solution.py:10
  68.3 0.0 all-reduce.2.cloned.1.call-update
  68.4 29.7 %all-reduce.2.cloned.1.call-done = f32[64,256]{1,0:T(8,128)} async-done(((f32[64,256]{1,0:T(8,128)}), f32[64,256]{1,0:T(8,128)}) %all-reduce.2.cloned.1.call-update) | async-done | bytes 65552 | tf_op jit(solution)/shard_map/psum | solution.py:11
  98.1 0.0 copy-done.1
  98.1 1.6 %fusion.2 = (bf16[64,256]{1,0:T(8,128)(2,1)S(1)}, f32[64,256]{1,0:T(8,128)}) fusion(f32[64,256]{1,0:T(8,128)} %all-reduce.2.cloned.1.call-done, bf16[64,256]{1,0:T(8,128)(2,1)S(1)} %copy-done.1), kind=kLoop, calls=%fused_computation.4 | loop fusion | flops 65536 | bytes 196608 | tf_op jit(solution)/shard_map/convert_element_type | solution.py:13
  99.6 30.8 %all_gather.7 = bf16[64,2048]{1,0:T(8,128)(2,1)S(1)} all-gather(bf16[64,256]{1,0:T(8,128)(2,1)S(1)} %get-tuple-element.2), channel_id=1, replica_groups=mesh['row'=4,'col'=8] {'col'}, dimensions={1}, use_global_device_ids=true | all-gather | bytes 294912 | tf_op jit(solution)/shard_map/all_gather | solution.py:16
  130.5 0.0 copy-done
  130.5 5.8 %multiply_convert_fusion = bf16[512,8192]{1,0:T(8,128)(2,1)} fusion(bf16[64,8192]{1,0:T(8,128)(2,1)S(1)} %copy-done, bf16[64,2048]{1,0:T(8,128)(2,1)S(1)} %all_gather.7, s32[]{:T(128)S(6)} %select_n.3), kind=kOutput, calls=%fused_computation | convolution fusion | flops 545259520 | bytes 9502724 | tf_op jit(solution)/shard_map/dot_general | solution.py:19
Async XLA Ops:
  7.2 123.3 %copy-start = (bf16[64,8192]{1,0:T(8,128)(2,1)S(1)}, bf16[64,8192]{1,0:T(8,128)(2,1)}, u32[]{:S(2)}) copy-start(bf16[64,8192]{1,0:T(8,128)(2,1)} %param.7) | copy-start | bytes 3145732
  7.2 55.0 %all-gather.2.cloned.1.call-start = ((), (), s32[]{:S(2)}) async-start(), calls=%async_computation | async-start | bytes 2359296 | tf_op jit(solution)/shard_map/all_gather | solution.py:9
  7.9 90.2 %copy-start.1 = (bf16[64,256]{1,0:T(8,128)(2,1)S(1)}, bf16[64,256]{1,0:T(8,128)(2,1)}, u32[]{:S(2)}) copy-start(bf16[64,256]{1,0:T(8,128)(2,1)} %param.6) | copy-start | bytes 98308
  7.9 90.2 %all-reduce.2.cloned.1.call-start = ((), (), s32[]{:S(2)}) async-start(), calls=%async_computation.1 | async-start | bytes 131072 | tf_op jit(solution)/shard_map/psum | solution.py:11
Sparse Core Ops, SparseCore 0:
  10.2 51.9 all-gather.1
  68.5 29.5 all-reduce.1
where the time goes:
time: 143 us
  waiting for transfers between devices  84.7 us (59%)
  blocking collectives  30.8 us (22%)
  between operations  14.1 us (10%)
  matrix products  11.9 us (8%)
  other arithmetic  1.55 us (1%)
    all_gather x1, waiting for transfers between devices, body(): block_rows = lax.all_gather(cot_solved, 'col', axis=1, tiled=True)  54.2 us
    all_gather x1, blocking collectives, body(): gathered = lax.all_gather(pulled_low, 'col', axis=1, tiled=True)  30.8 us
    psum x1, waiting for transfers between devices, body(): pulled = lax.psum(partial_sum, 'row')  29.7 us
    dot_general x1, matrix products, body(): jnp.dot(block_rows, inverse_slab, preferred_element_type=jnp.float32)  6.12 us
    dot_general x1, matrix products, body(): lax.dot_general(needed, solved_panel, (((0,), (0,)), ((), ())), preferred...  5.78 us
  transfers between devices with their start and end apart: 2, of which 2 were waited for; matrix products, arithmetic and copies ran while one was open for 0% of the time, Pallas kernels for 0%

commit v1 on v0

v1 whole, which is shorter than its diff:
```python
import functools

import jax
import jax.numpy as jnp
from jax import lax
from jax.experimental import pallas as pl
from jax.experimental.pallas import tpu as pltpu
from jax.sharding import PartitionSpec as P

MESH = pl.DeviceIdType.MESH
PIECE = 16


def when(*conds):
    traced = None
    for cond in conds:
        if cond is not True:
            traced = cond if traced is None else jnp.logical_and(traced, cond)
    if traced is None:
        return lambda body: body()
    return pl.when(traced)


def pull_kernel(n_row, n_col, pieces, chunks,
                inverse_ref, cot_ref, needed_ref, pulled_ref,
                gathered, inverse, part, arrived, low,
                load_sem, own_sem, recv_sem, send_sem, sum_send, sum_recv,
                total_send, total_recv, low_send, low_recv):
    row, col = lax.axis_index("row"), lax.axis_index("col")
    line = n_col // 2
    z, x = col // 2, col % 2
    other = 1 - x
    factor = n_col // n_row
    depth = cot_ref.shape[1]
    rows = cot_ref.shape[0] // chunks
    balance = line >= 4

    def load_inverse(at, slot):
        span = pl.ds(pl.multiple_of(at * depth, depth), depth)
        return pltpu.make_async_copy(inverse_ref.at[span], inverse.at[span], load_sem.at[slot])

    own = pltpu.make_async_copy(cot_ref, gathered.at[col], own_sem)
    own.start()

    barrier = pltpu.get_barrier_semaphore()

    def greet(to_row, to_col):
        pl.semaphore_signal(barrier, inc=1, device_id=(to_row, to_col), device_id_type=MESH)

    has_down, has_up = z > 0, z < line - 1
    greet(row, z * 2 + other)
    pl.when(has_down)(lambda: greet(row, col - 2))
    pl.when(has_up)(lambda: greet(row, col + 2))
    for step in range(1, n_row):
        greet(lax.rem(row + step, n_row), col)

    for at in range(n_col):
        load_inverse(lax.rem(col + at, n_col), lax.rem(col + at, n_col)).start()
    own.wait()
    pl.semaphore_wait(barrier, n_row + has_down.astype(jnp.int32) + has_up.astype(jnp.int32))

    def move(block, chunk, stream, to_col):
        piece = gathered.at[block, pl.ds(chunk * rows, rows), :]
        return pltpu.make_async_remote_copy(
            src_ref=piece, dst_ref=piece,
            send_sem=send_sem.at[stream, block, chunk], recv_sem=recv_sem.at[block, chunk],
            device_id=(row, to_col), device_id_type=MESH)

    UP, DOWN, ACROSS = 0, 1, 2
    half = chunks // 2
    sends = []

    def send(stream, block, chunk, *conds):
        to_col = {UP: col + 2, DOWN: col - 2, ACROSS: z * 2 + other}[stream]
        when(*conds)(lambda: move(block, chunk, stream, to_col).start())
        sends.append((stream, block, chunk, to_col, conds))

    def receive(block, chunk, *conds):
        when(*conds)(lambda: move(block, chunk, ACROSS, z * 2 + other).wait_recv())

    def across_ok(at_z, of_z, chunk):
        if not balance:
            return ()
        conds = [
            jnp.logical_not(jnp.logical_and(at_z == 1, of_z == 0)),
            jnp.logical_not(jnp.logical_and(at_z == line - 2, of_z == line - 1)),
        ]
        if chunk >= half:
            conds.append(jnp.logical_not(jnp.logical_and(at_z == 0, of_z == 1)))
            conds.append(jnp.logical_not(jnp.logical_and(at_z == line - 1, of_z == line - 2)))
        return conds

    def multiply(block):
        load_inverse(block, block).wait()
        span = pl.ds(pl.multiple_of(block * depth, depth), depth)
        part[...] += jnp.dot(gathered[block], inverse[span, :], preferred_element_type=jnp.float32)

    def take(block, *conds):
        @when(*conds)
        def _():
            for chunk in range(chunks):
                receive(block, chunk)
            multiply(block)

    def finish_pair(step):
        below, above = z - 1 - step, z + 1 + step
        late = balance and step == 0
        take(below * 2 + other, below >= 0, z != line - 1 if late else True)
        take(above * 2 + other, above < line, z != 0 if late else True)

    for chunk in range(chunks):
        send(UP, col, chunk, has_up)
        send(DOWN, col, chunk, has_down)
        send(ACROSS, col, chunk)
    part[...] = jnp.zeros_like(part)
    multiply(col)

    for step in range(line - 1):
        below, above = z - 1 - step, z + 1 + step
        from_below, from_above = below >= 0, above < line
        below_col, above_col = below * 2 + x, above * 2 + x
        for chunk in range(chunks):
            receive(below_col, chunk, from_below)
            send(UP, below_col, chunk, from_below, has_up)
            send(ACROSS, below_col, chunk, from_below, *across_ok(z, below, chunk))
            receive(above_col, chunk, from_above)
            send(DOWN, above_col, chunk, from_above, has_down)
            send(ACROSS, above_col, chunk, from_above, *across_ok(z, above, chunk))
        if step == line - 2 and balance:
            for chunk in range(half, chunks):
                send(DOWN, z * 2 + other, chunk, z == 1)
                send(UP, z * 2 + other, chunk, z == line - 2)
        pl.when(from_below)(lambda: multiply(below_col))
        pl.when(from_above)(lambda: multiply(above_col))
        if step == 0:
            for chunk in range(chunks):
                receive(z * 2 + other, chunk)
                if balance:
                    send(UP, z * 2 + other, chunk, z == 0)
                    send(DOWN, z * 2 + other, chunk, z == line - 1)
            multiply(z * 2 + other)
        else:
            finish_pair(step - 1)
    finish_pair(line - 2)
    if balance:
        take(z * 2 + 2 + other, z == 0)
        take(z * 2 - 2 + other, z == line - 1)

    def sum_copy(piece, source):
        return pltpu.make_async_remote_copy(
            src_ref=part.at[pl.ds(piece * PIECE, PIECE), :], dst_ref=arrived.at[source],
            send_sem=sum_send.at[piece], recv_sem=sum_recv.at[source],
            device_id=(piece, col), device_id_type=MESH)

    for piece in range(pieces):
        pl.when(row != piece)(lambda: sum_copy(piece, row).start())

    def total_copy(piece, to_row):
        span = pl.ds(pl.multiple_of(piece * PIECE, PIECE), PIECE)
        return pltpu.make_async_remote_copy(
            src_ref=pulled_ref.at[span, :], dst_ref=pulled_ref.at[span, :],
            send_sem=total_send.at[to_row], recv_sem=total_recv.at[piece],
            device_id=(to_row, col), device_id_type=MESH)

    def low_copy(piece, slot, to_row, to_col):
        span = pl.ds(pl.multiple_of(piece * PIECE, PIECE), PIECE)
        return pltpu.make_async_remote_copy(
            src_ref=low, dst_ref=needed_ref.at[slot, span, :],
            send_sem=low_send.at[to_col], recv_sem=low_recv.at[slot, piece],
            device_id=(to_row, to_col), device_id_type=MESH)

    user, slot = col // factor, col % factor

    @pl.when(row < pieces)
    def _():
        span = pl.ds(pl.multiple_of(row * PIECE, PIECE), PIECE)
        for step in range(1, n_row):
            source = lax.rem(row + step, n_row)
            sum_copy(row, source).wait_recv()
        arrived[row] = part[span, :]
        total = arrived[0]
        for source in range(1, n_row):
            total = total + arrived[source]
        low[...] = total.astype(jnp.bfloat16)
        pulled_ref[span, :] = total
        for to_col in range(n_col):
            mine = jnp.logical_and(user == row, col == to_col)
            pl.when(jnp.logical_not(mine))(lambda: low_copy(row, slot, user, to_col).start())
        for step in range(1, n_row):
            total_copy(row, lax.rem(row + step, n_row)).start()

        @pl.when(user == row)
        def _():
            needed_ref[slot, span, :] = low[...]

    for piece in range(pieces):
        pl.when(row != piece)(lambda: total_copy(piece, row).wait_recv())
        for at in range(factor):
            mine = jnp.logical_and(row == piece, col == factor * row + at)
            pl.when(jnp.logical_not(mine))(lambda: low_copy(piece, at, row, col).wait_recv())

    for stream, block, chunk, to_col, conds in sends:
        when(*conds)(lambda: move(block, chunk, stream, to_col).wait_send())
    for piece in range(pieces):
        pl.when(row != piece)(lambda: sum_copy(piece, row).wait_send())

    @pl.when(row < pieces)
    def _():
        for to_col in range(n_col):
            mine = jnp.logical_and(user == row, col == to_col)
            pl.when(jnp.logical_not(mine))(lambda: low_copy(row, slot, user, to_col).wait_send())
        for step in range(1, n_row):
            total_copy(row, lax.rem(row + step, n_row)).wait_send()


def operator_kernel(needed_ref, panel_ref, direct_ref, pulled_ref, factor_ref, operator_ref):
    scale = 1.0 / jnp.sqrt(jnp.float32(2.0))

    @pl.when(pl.program_id(0) == 0)
    def _():
        factor_ref[...] = (direct_ref[...].astype(jnp.float32) + pulled_ref[...]) * scale

    width = needed_ref.shape[2]
    for at in range(needed_ref.shape[0]):
        product = lax.dot_general(
            needed_ref[at], panel_ref[...], (((0,), (0,)), ((), ())), preferred_element_type=jnp.float32)
        operator_ref[at * width:(at + 1) * width, :] = (product * -scale).astype(jnp.bfloat16)


def body(n_row, n_col, inverse_slab, cot_solved, cot_direct, solved_panel):
    n_states, width = inverse_slab.shape
    columns, depth = cot_solved.shape
    factor = n_col // n_row
    pieces = min(n_row, columns // PIECE)
    chunks = 4 if depth >= 1024 else 1
    any_space = pl.BlockSpec(memory_space=pl.ANY)
    vmem = pl.BlockSpec(memory_space=pltpu.VMEM)
    dma = pltpu.SemaphoreType.DMA
    needed, pulled = pl.pallas_call(
        functools.partial(pull_kernel, n_row, n_col, pieces, chunks),
        out_shape=(
            jax.ShapeDtypeStruct((factor, columns, width), jnp.bfloat16),
            jax.ShapeDtypeStruct((columns, width), jnp.float32),
        ),
        in_specs=[any_space, any_space],
        out_specs=(vmem, vmem),
        scratch_shapes=[
            pltpu.VMEM((n_col, columns, depth), jnp.bfloat16),
            pltpu.VMEM((n_states, width), jnp.bfloat16),
            pltpu.VMEM((columns, width), jnp.float32),
            pltpu.VMEM((n_row, PIECE, width), jnp.float32),
            pltpu.VMEM((PIECE, width), jnp.bfloat16),
            dma((n_col,)), dma, dma((n_col, chunks)), dma((3, n_col, chunks)),
            dma((pieces,)), dma((n_row,)),
            dma((n_row,)), dma((pieces,)), dma((n_col,)), dma((factor, pieces)),
        ],
        compiler_params=pltpu.CompilerParams(
            collective_id=0, has_side_effects=True, vmem_limit_bytes=48 * 2**20),
        cost_estimate=pl.CostEstimate(
            flops=2 * columns * n_states * width, bytes_accessed=2 * n_states * width, transcendentals=0),
        name="pull",
    )(inverse_slab, cot_solved)

    panel_width = solved_panel.shape[1]
    tile = min(panel_width, 1024)
    return pl.pallas_call(
        operator_kernel,
        grid=(panel_width // tile,),
        out_shape=(
            jax.ShapeDtypeStruct((columns, width), jnp.float32),
            jax.ShapeDtypeStruct((factor * width, panel_width), jnp.bfloat16),
        ),
        in_specs=[
            pl.BlockSpec((factor, columns, width), lambda i: (0, 0, 0)),
            pl.BlockSpec((columns, tile), lambda i: (0, i)),
            pl.BlockSpec((columns, width), lambda i: (0, 0)),
            pl.BlockSpec((columns, width), lambda i: (0, 0)),
        ],
        out_specs=(
            pl.BlockSpec((columns, width), lambda i: (0, 0)),
            pl.BlockSpec((factor * width, tile), lambda i: (0, i)),
        ),
        compiler_params=pltpu.CompilerParams(vmem_limit_bytes=32 * 2**20),
        cost_estimate=pl.CostEstimate(
            flops=2 * columns * factor * width * panel_width,
            bytes_accessed=2 * factor * width * panel_width, transcendentals=0),
        name="operator",
    )(needed, solved_panel, cot_direct, pulled)


def solution(mesh):
    n_row, n_col = mesh.shape["row"], mesh.shape["col"]
    in_specs = (P("row", "col"), P(None, ("row", "col")), P(None, "col"), P(None, "col"))
    out_specs = (P(None, "col"), P("row", "col"))
    return jax.shard_map(
        functools.partial(body, n_row, n_col),
        mesh=mesh, in_specs=in_specs, out_specs=out_specs, check_vma=False)
```

time: 143 us -> 43 us (0.30)
  waiting for transfers between devices: 84.7 us -> 0 us
  Pallas kernels: 0 us -> 41 us
  blocking collectives: 30.8 us -> 0 us
  between operations: 14.1 us -> 0.66 us
  matrix products: 11.9 us -> 0 us
  other arithmetic: 1.55 us -> 0 us
    all_gather x1 -> x0, waiting for transfers between devices: 54.2 us -> none  [body(): block_rows = lax.all_gather(cot_solved, 'col', axis=1, tiled=True)]
    pallas_call x0 -> x2, Pallas kernels: none -> 41 us  [the longest x1 34.8 us: body(): pl.pallas_call(functools.partial(pull_kernel, n_row, n_col, pieces, chunk...]
    all_gather x1 -> x0, blocking collectives: 30.8 us -> none  [body(): gathered = lax.all_gather(pulled_low, 'col', axis=1, tiled=True)]
    psum x1 -> x0, waiting for transfers between devices: 29.7 us -> none  [body(): pulled = lax.psum(partial_sum, 'row')]
    dot_general x2 -> x0, matrix products: 11.9 us -> none  [the longest x1 6.12 us: body(): jnp.dot(block_rows, inverse_slab, preferred_element_type=jnp.float32)]
    convert_element_type x1 -> x0, other arithmetic: 1.55 us -> none  [body(): pulled_low = pulled.astype(jnp.bfloat16)]
  transfers between devices with their start and end apart: 2 -> 0, of which waited for: 2 -> 0; matrix products, arithmetic and copies ran while one was open for 0% -> 0% of each run, Pallas kernels for 0% -> 0%
where the time goes in v1:
time: 43 us; the launch traced here: 42.6 us
  Pallas kernels  41 us (95%)
  local copies, waits for them, and re-layouts  0.95 us (2%)
  between operations  0.66 us (2%)
    pallas_call x1, Pallas kernels, body(): pl.pallas_call(functools.partial(pull_kernel, n_row, n_col, pieces, chunk...  34.8 us
    pallas_call x1, Pallas kernels, body(): pl.pallas_call(operator_kernel, grid=(panel_width // tile,), out_shape=(j...  6.26 us
    unnamed x6, local copies, waits for them, and re-layouts  0.95 us

profile of v1, /device:TPU:0, one launch (start us, length us, event | category | flops | bytes accessed | tf_op | source)
XLA Modules:
  0.0 42.6 jit_solution(15481455017328725853)
XLA Ops:
  0.6 0.0 copy-start
  0.6 0.9 %copy-done = bf16[64,2048]{1,0:T(8,128)(2,1)S(1)} copy-done((bf16[64,2048]{1,0:T(8,128)(2,1)S(1)}, bf16[64,2048]{1,0:T(8,128)(2,1)}, u32[]{:S(2)}) %copy-start) | copy-done | bytes 262168
  1.6 0.0 copy-start.1
  1.6 0.0 copy-start.2
  1.6 34.8 %pull.1 = (bf16[2,64,256]{2,1,0:T(8,128)(2,1)S(1)}, f32[64,256]{1,0:T(8,128)S(1)}) custom-call(bf16[16384,256]{1,0:T(8,128)(2,1)} %inverse_ref.1, bf16[64,2048]{1,0:T(8,128)(2,1)S(1)} %copy-done), custom_call_target="tpu_custom_call" | custom-call | flops 536870912 | bytes 8388608 | tf_op jit(solution)/shard_map/pull/pallas_call | solution.py:239
  36.4 0.0 copy-done.1
  36.4 0.0 copy-done.2
  36.4 6.3 %operator.1 = (f32[64,256]{1,0:T(8,128)}, bf16[512,8192]{1,0:T(8,128)(2,1)}) custom-call(bf16[2,64,256]{2,1,0:T(8,128)(2,1)S(1)} %get-tuple-element.4.needed_ref, bf16[64,8192]{1,0:T(8,128)(2,1)S(1)} %copy-done.1, bf16[64,256]{1,0:T(8,128)(2,1)S(1)} %copy-done.2, f32[64,256]{1,0:T(8,128)S(1)} %get-tuple-element.5.pulled_ref), custom_call_target="tpu_custom_call" | custom-call | flops 536870912 | bytes 8388608 | tf_op jit(solution)/shard_map/operator/pallas_call | solution.py:266
Async XLA Ops:
  0.6 1.0 %copy-start = (bf16[64,2048]{1,0:T(8,128)(2,1)S(1)}, bf16[64,2048]{1,0:T(8,128)(2,1)}, u32[]{:S(2)}) copy-start(bf16[64,2048]{1,0:T(8,128)(2,1)} %cot_ref.1) | copy-start | bytes 786436
  1.6 34.8 %copy-start.1 = (bf16[64,8192]{1,0:T(8,128)(2,1)S(1)}, bf16[64,8192]{1,0:T(8,128)(2,1)}, u32[]{:S(2)}) copy-start(bf16[64,8192]{1,0:T(8,128)(2,1)} %panel_ref.1) | copy-start | bytes 3145732
  1.6 34.8 %copy-start.2 = (bf16[64,256]{1,0:T(8,128)(2,1)S(1)}, bf16[64,256]{1,0:T(8,128)(2,1)}, u32[]{:S(2)}) copy-start(bf16[64,256]{1,0:T(8,128)(2,1)} %direct_ref.1) | copy-start | bytes 98308

commit v2 on v1

v2 whole, which is shorter than its diff:
```python
import functools

import jax
import jax.numpy as jnp
from jax import lax
from jax.experimental import pallas as pl
from jax.experimental.pallas import tpu as pltpu
from jax.sharding import PartitionSpec as P

MESH = pl.DeviceIdType.MESH
PIECE = 16


def when(*conds):
    traced = None
    for cond in conds:
        if cond is not True:
            traced = cond if traced is None else jnp.logical_and(traced, cond)
    if traced is None:
        return lambda body: body()
    return pl.when(traced)


def pull_kernel(n_row, n_col, pieces, chunks,
                inverse_ref, cot_ref, needed_ref, pulled_ref,
                gathered, inverse, part, arrived, low,
                load_sem, own_sem, recv_sem, send_sem, sum_send, sum_recv,
                total_send, total_recv, low_send, low_recv):
    row, col = lax.axis_index("row"), lax.axis_index("col")
    line = n_col // 2
    z, x = col // 2, col % 2
    other = 1 - x
    pair = z * 2 + other
    factor = n_col // n_row
    depth = cot_ref.shape[1]
    span_of = depth // chunks
    balance = line >= 4
    half = chunks // 2
    window = min(2, chunks)
    ticks = (line - 1) * chunks
    has_down, has_up = z > 0, z < line - 1

    def load_inverse(block):
        span = pl.ds(pl.multiple_of(block * depth, depth), depth)
        return pltpu.make_async_copy(inverse_ref.at[span], inverse.at[span], load_sem.at[block])

    def load_own(chunk):
        return pltpu.make_async_copy(
            cot_ref.at[:, pl.ds(chunk * span_of, span_of)], gathered.at[col, chunk], own_sem.at[chunk])

    for chunk in range(chunks):
        load_own(chunk).start()

    barrier = pltpu.get_barrier_semaphore()

    def greet(to_row, to_col):
        pl.semaphore_signal(barrier, inc=1, device_id=(to_row, to_col), device_id_type=MESH)

    greet(row, pair)
    pl.when(has_down)(lambda: greet(row, col - 2))
    pl.when(has_up)(lambda: greet(row, col + 2))
    for step in range(1, n_row):
        greet(lax.rem(row + step, n_row), col)

    for at in range(n_col):
        load_inverse(lax.rem(col + at, n_col)).start()
    part[...] = jnp.zeros_like(part)
    for chunk in range(chunks):
        load_own(chunk).wait()
    pl.semaphore_wait(barrier, n_row + has_down.astype(jnp.int32) + has_up.astype(jnp.int32))

    UP, DOWN, ACROSS = 0, 1, 2
    target = {UP: col + 2, DOWN: col - 2, ACROSS: pair}

    def move(stream, block, chunk):
        piece = gathered.at[block, chunk]
        return pltpu.make_async_remote_copy(
            src_ref=piece, dst_ref=piece,
            send_sem=send_sem.at[stream, block, chunk], recv_sem=recv_sem.at[block, chunk],
            device_id=(row, target[stream]), device_id_type=MESH)

    def receive(block, chunk, *conds):
        when(*conds)(lambda: move(ACROSS, block, chunk).wait_recv())

    def multiply(block, chunk, *conds):
        @when(*conds)
        def _():
            if chunk == 0:
                load_inverse(block).wait()
            span = pl.ds(pl.multiple_of(block * depth + chunk * span_of, span_of), span_of)
            part[...] += jnp.dot(
                gathered[block, chunk], inverse[span, :], preferred_element_type=jnp.float32)

    def entry(stream, at):
        step, chunk = divmod(at, chunks)
        leaves, sign = (has_up, -1) if stream == UP else (has_down, 1)
        start, before_end = (0, line - 2) if stream == UP else (line - 1, 1)
        if step == 0:
            return col, chunk, (leaves,)
        if step == line - 1:
            if not balance or chunk + half >= chunks:
                return None
            return pair, chunk + half, (z == before_end,)
        source = z + sign * step
        inside = source >= 0 if stream == UP else source < line
        if step == 1 and balance:
            first = z == start
            return jnp.where(first, pair, source * 2 + x), chunk, (leaves, jnp.logical_or(first, inside))
        return source * 2 + x, chunk, (leaves, inside)

    open_sends = []

    def start(stream, block, chunk, *conds):
        when(*conds)(lambda: move(stream, block, chunk).start())

    def finish(stream, block, chunk, *conds):
        when(*conds)(lambda: move(stream, block, chunk).wait_send())

    def advance(stream, tick):
        new = entry(stream, tick + window)
        if new is None:
            return
        if tick >= 0:
            old = entry(stream, tick)
            finish(stream, old[0], old[1], *old[2])
            open_sends.remove((stream, tick))
        start(stream, new[0], new[1], *new[2])
        open_sends.append((stream, tick + window))

    across = []

    def start_across(block, chunk, *conds):
        start(ACROSS, block, chunk, *conds)
        across.append((block, chunk, conds))

    def across_ok(of_z, chunk):
        if not balance:
            return ()
        conds = [
            jnp.logical_not(jnp.logical_and(z == 1, of_z == 0)),
            jnp.logical_not(jnp.logical_and(z == line - 2, of_z == line - 1)),
        ]
        if chunk >= half:
            conds.append(jnp.logical_not(jnp.logical_and(z == 0, of_z == 1)))
            conds.append(jnp.logical_not(jnp.logical_and(z == line - 1, of_z == line - 2)))
        return conds

    def pass_across(step, chunk):
        below, above = z - 1 - step, z + 1 + step
        start_across(below * 2 + x, chunk, below >= 0, *across_ok(below, chunk))
        start_across(above * 2 + x, chunk, above < line, *across_ok(above, chunk))

    def take(block, chunk, *conds):
        receive(block, chunk, *conds)
        multiply(block, chunk, *conds)

    def take_pair(step, chunk):
        below, above = z - 1 - step, z + 1 + step
        late = balance and step == 0 and chunk >= half
        take(below * 2 + other, chunk, below >= 0, z != line - 1 if late else True)
        take(above * 2 + other, chunk, above < line, z != 0 if late else True)

    for chunk in range(window):
        advance(UP, chunk - window)
        advance(DOWN, chunk - window)
        start_across(col, chunk)
    for chunk in range(chunks):
        multiply(col, chunk)

    for tick in range(ticks):
        step, chunk = divmod(tick, chunks)
        below, above = z - 1 - step, z + 1 + step
        receive(below * 2 + x, chunk, below >= 0)
        advance(UP, tick)
        receive(above * 2 + x, chunk, above < line)
        advance(DOWN, tick)
        if tick + window < chunks:
            start_across(col, tick + window)
        if 0 <= tick - window < chunks:
            pass_across(0, tick - window)
        if step >= 1:
            pass_across(step, chunk)
        multiply(below * 2 + x, chunk, below >= 0)
        multiply(above * 2 + x, chunk, above < line)
        if step == 0:
            take(pair, chunk)
        if step >= 2:
            take_pair(step - 2, chunk)
    for tick in range(ticks, ticks + chunks - half - window):
        advance(UP, tick)
        advance(DOWN, tick)
    for step in range(max(line - 3, 0), line - 1):
        for chunk in range(chunks):
            take_pair(step, chunk)
            if step == line - 2 and balance and chunk >= half:
                take(2 + other, chunk, z == 0)
                take((line - 2) * 2 + other, chunk, z == line - 1)

    def sum_copy(piece, source):
        return pltpu.make_async_remote_copy(
            src_ref=part.at[pl.ds(piece * PIECE, PIECE), :], dst_ref=arrived.at[source],
            send_sem=sum_send.at[piece], recv_sem=sum_recv.at[source],
            device_id=(piece, col), device_id_type=MESH)

    for piece in range(pieces):
        pl.when(row != piece)(lambda: sum_copy(piece, row).start())

    def total_copy(piece, to_row):
        span = pl.ds(pl.multiple_of(piece * PIECE, PIECE), PIECE)
        return pltpu.make_async_remote_copy(
            src_ref=pulled_ref.at[span, :], dst_ref=pulled_ref.at[span, :],
            send_sem=total_send.at[to_row], recv_sem=total_recv.at[piece],
            device_id=(to_row, col), device_id_type=MESH)

    def low_copy(piece, slot, to_row, to_col):
        span = pl.ds(pl.multiple_of(piece * PIECE, PIECE), PIECE)
        return pltpu.make_async_remote_copy(
            src_ref=low, dst_ref=needed_ref.at[slot, span, :],
            send_sem=low_send.at[to_col], recv_sem=low_recv.at[slot, piece],
            device_id=(to_row, to_col), device_id_type=MESH)

    user, slot = col // factor, col % factor

    @pl.when(row < pieces)
    def _():
        span = pl.ds(pl.multiple_of(row * PIECE, PIECE), PIECE)
        for step in range(1, n_row):
            source = lax.rem(row + step, n_row)
            sum_copy(row, source).wait_recv()
        arrived[row] = part[span, :]
        total = arrived[0]
        for source in range(1, n_row):
            total = total + arrived[source]
        low[...] = total.astype(jnp.bfloat16)
        pulled_ref[span, :] = total
        for to_col in range(n_col):
            mine = jnp.logical_and(user == row, col == to_col)
            pl.when(jnp.logical_not(mine))(lambda: low_copy(row, slot, user, to_col).start())
        for step in range(1, n_row):
            total_copy(row, lax.rem(row + step, n_row)).start()

        @pl.when(user == row)
        def _():
            needed_ref[slot, span, :] = low[...]

    for piece in range(pieces):
        pl.when(row != piece)(lambda: total_copy(piece, row).wait_recv())
        for at in range(factor):
            mine = jnp.logical_and(row == piece, col == factor * row + at)
            pl.when(jnp.logical_not(mine))(lambda: low_copy(piece, at, row, col).wait_recv())

    for stream, at in open_sends:
        block, chunk, conds = entry(stream, at)
        finish(stream, block, chunk, *conds)
    for block, chunk, conds in across:
        finish(ACROSS, block, chunk, *conds)
    for piece in range(pieces):
        pl.when(row != piece)(lambda: sum_copy(piece, row).wait_send())

    @pl.when(row < pieces)
    def _():
        for to_col in range(n_col):
            mine = jnp.logical_and(user == row, col == to_col)
            pl.when(jnp.logical_not(mine))(lambda: low_copy(row, slot, user, to_col).wait_send())
        for step in range(1, n_row):
            total_copy(row, lax.rem(row + step, n_row)).wait_send()


def operator_kernel(tile, needed_ref, panel_ref, direct_ref, pulled_ref, factor_ref, operator_ref,
                    left, factor, result, factor_sem, result_sem):
    scale = 1.0 / jnp.sqrt(jnp.float32(2.0))
    width = needed_ref.shape[2]
    for at in range(needed_ref.shape[0]):
        left[at * width:(at + 1) * width, :] = needed_ref[at].T

    def store(at):
        span = pl.ds(at * tile, tile)
        return pltpu.make_async_copy(result.at[at], operator_ref.at[:, span], result_sem.at[at])

    tiles = panel_ref.shape[1] // tile
    for at in range(tiles):
        product = jnp.dot(
            left[...], panel_ref[:, at * tile:(at + 1) * tile], preferred_element_type=jnp.float32)
        result[at] = (product * -scale).astype(jnp.bfloat16)
        store(at).start()
        if at == 0:
            factor[...] = (direct_ref[...].astype(jnp.float32) + pulled_ref[...]) * scale
            out = pltpu.make_async_copy(factor, factor_ref, factor_sem)
            out.start()
    for at in range(tiles):
        store(at).wait()
    out.wait()


def body(n_row, n_col, inverse_slab, cot_solved, cot_direct, solved_panel):
    n_states, width = inverse_slab.shape
    columns, depth = cot_solved.shape
    factor = n_col // n_row
    pieces = min(n_row, columns // PIECE)
    chunks = 4 if depth >= 1024 else 1
    hbm = pl.BlockSpec(memory_space=pltpu.HBM)
    vmem = pl.BlockSpec(memory_space=pltpu.VMEM)
    dma = pltpu.SemaphoreType.DMA
    needed, pulled = pl.pallas_call(
        functools.partial(pull_kernel, n_row, n_col, pieces, chunks),
        out_shape=(
            jax.ShapeDtypeStruct((factor, columns, width), jnp.bfloat16),
            jax.ShapeDtypeStruct((columns, width), jnp.float32),
        ),
        in_specs=[hbm, hbm],
        out_specs=(vmem, vmem),
        scratch_shapes=[
            pltpu.VMEM((n_col, chunks, columns, depth // chunks), jnp.bfloat16),
            pltpu.VMEM((n_states, width), jnp.bfloat16),
            pltpu.VMEM((columns, width), jnp.float32),
            pltpu.VMEM((n_row, PIECE, width), jnp.float32),
            pltpu.VMEM((PIECE, width), jnp.bfloat16),
            dma((n_col,)), dma((chunks,)), dma((n_col, chunks)), dma((3, n_col, chunks)),
            dma((pieces,)), dma((n_row,)),
            dma((n_row,)), dma((pieces,)), dma((n_col,)), dma((factor, pieces)),
        ],
        compiler_params=pltpu.CompilerParams(
            collective_id=0, has_side_effects=True, vmem_limit_bytes=48 * 2**20),
        cost_estimate=pl.CostEstimate(
            flops=2 * columns * n_states * width, bytes_accessed=2 * n_states * width, transcendentals=0),
        name="pull",
    )(inverse_slab, cot_solved)

    panel_width = solved_panel.shape[1]
    tile = min(panel_width, 512)
    tiles = panel_width // tile
    return pl.pallas_call(
        functools.partial(operator_kernel, tile),
        out_shape=(
            jax.ShapeDtypeStruct((columns, width), jnp.float32),
            jax.ShapeDtypeStruct((factor * width, panel_width), jnp.bfloat16),
        ),
        in_specs=[vmem] * 4,
        out_specs=(hbm, hbm),
        scratch_shapes=[
            pltpu.VMEM((factor * width, columns), jnp.bfloat16),
            pltpu.VMEM((columns, width), jnp.float32),
            pltpu.VMEM((tiles, factor * width, tile), jnp.bfloat16),
            dma, dma((tiles,)),
        ],
        compiler_params=pltpu.CompilerParams(vmem_limit_bytes=32 * 2**20),
        cost_estimate=pl.CostEstimate(
            flops=2 * columns * factor * width * panel_width,
            bytes_accessed=2 * factor * width * panel_width, transcendentals=0),
        name="operator",
    )(needed, solved_panel, cot_direct, pulled)


def solution(mesh):
    n_row, n_col = mesh.shape["row"], mesh.shape["col"]
    in_specs = (P("row", "col"), P(None, ("row", "col")), P(None, "col"), P(None, "col"))
    out_specs = (P(None, "col"), P("row", "col"))
    return jax.shard_map(
        functools.partial(body, n_row, n_col),
        mesh=mesh, in_specs=in_specs, out_specs=out_specs, check_vma=False)
```

time: 43 us -> 43.3 us (level)
  Pallas kernels: 41 us -> 41.5 us
    pallas_call x1, Pallas kernels: 34.8 us -> 37.7 us  [body(): pl.pallas_call(functools.partial(pull_kernel, n_row, n_col, pieces, chunk...]
    pallas_call x1, Pallas kernels: 6.26 us -> 3.78 us  [body(): pl.pallas_call(functools.partial(operator_kernel, tile), out_shape=(jax.S...]
where the time goes in v2:
time: 43.3 us; the launch traced here: 43.1 us
  Pallas kernels  41.5 us (96%)
  local copies, waits for them, and re-layouts  0.95 us (2%)
  between operations  0.66 us (2%)
    pallas_call x1, Pallas kernels, body(): pl.pallas_call(functools.partial(pull_kernel, n_row, n_col, pieces, chunk...  37.7 us
    pallas_call x1, Pallas kernels, body(): pl.pallas_call(functools.partial(operator_kernel, tile), out_shape=(jax.S...  3.78 us
    unnamed x6, local copies, waits for them, and re-layouts  0.95 us

profile of v2, /device:TPU:0, one launch (start us, length us, event | category | flops | bytes accessed | tf_op | source)
XLA Modules:
  0.0 43.1 jit_solution(14340753234016277927)
XLA Ops:
  0.6 0.0 copy-start
  0.6 0.9 %copy-done = bf16[64,2048]{1,0:T(8,128)(2,1)S(1)} copy-done((bf16[64,2048]{1,0:T(8,128)(2,1)S(1)}, bf16[64,2048]{1,0:T(8,128)(2,1)}, u32[]{:S(2)}) %copy-start) | copy-done | bytes 262168
  1.6 0.0 copy-start.1
  1.6 0.0 copy-start.2
  1.6 37.7 %pull.1 = (bf16[2,64,256]{2,1,0:T(8,128)(2,1)S(1)}, f32[64,256]{1,0:T(8,128)S(1)}) custom-call(bf16[16384,256]{1,0:T(8,128)(2,1)} %inverse_ref.1, bf16[64,2048]{1,0:T(8,128)(2,1)S(1)} %copy-done), custom_call_target="tpu_custom_call" | custom-call | flops 536870912 | bytes 8388608 | tf_op jit(solution)/shard_map/pull/pallas_call | solution.py:304
  39.3 0.0 copy-done.1
  39.3 0.0 copy-done.2
  39.3 3.8 %operator.1 = (f32[64,256]{1,0:T(8,128)}, bf16[512,8192]{1,0:T(8,128)(2,1)}) custom-call(bf16[2,64,256]{2,1,0:T(8,128)(2,1)S(1)} %get-tuple-element.4.needed_ref, bf16[64,8192]{1,0:T(8,128)(2,1)S(1)} %copy-done.1, bf16[64,256]{1,0:T(8,128)(2,1)S(1)} %copy-done.2, f32[64,256]{1,0:T(8,128)S(1)} %get-tuple-element.5.pulled_ref), custom_call_target="tpu_custom_call" | custom-call | flops 536870912 | bytes 8388608 | tf_op jit(solution)/shard_map/operator/pallas_call | solution.py:332
Async XLA Ops:
  0.6 1.0 %copy-start = (bf16[64,2048]{1,0:T(8,128)(2,1)S(1)}, bf16[64,2048]{1,0:T(8,128)(2,1)}, u32[]{:S(2)}) copy-start(bf16[64,2048]{1,0:T(8,128)(2,1)} %cot_ref.1) | copy-start | bytes 786436
  1.6 37.7 %copy-start.1 = (bf16[64,8192]{1,0:T(8,128)(2,1)S(1)}, bf16[64,8192]{1,0:T(8,128)(2,1)}, u32[]{:S(2)}) copy-start(bf16[64,8192]{1,0:T(8,128)(2,1)} %panel_ref.1) | copy-start | bytes 3145732
  1.6 37.8 %copy-start.2 = (bf16[64,256]{1,0:T(8,128)(2,1)S(1)}, bf16[64,256]{1,0:T(8,128)(2,1)}, u32[]{:S(2)}) copy-start(bf16[64,256]{1,0:T(8,128)(2,1)} %direct_ref.1) | copy-start | bytes 98308

commit v3 on v2

--- a/solution.py
+++ b/solution.py
@@ -36,8 +36,6 @@
     span_of = depth // chunks
     balance = line >= 4
     half = chunks // 2
-    window = min(2, chunks)
-    ticks = (line - 1) * chunks
     has_down, has_up = z > 0, z < line - 1
 
     def load_inverse(block):
@@ -82,119 +80,79 @@
     def receive(block, chunk, *conds):
         when(*conds)(lambda: move(ACROSS, block, chunk).wait_recv())
 
-    def multiply(block, chunk, *conds):
-        @when(*conds)
-        def _():
-            if chunk == 0:
-                load_inverse(block).wait()
+    def multiply(block):
+        load_inverse(block).wait()
+        total = part[...]
+        for chunk in range(chunks):
             span = pl.ds(pl.multiple_of(block * depth + chunk * span_of, span_of), span_of)
-            part[...] += jnp.dot(
+            total += jnp.dot(
                 gathered[block, chunk], inverse[span, :], preferred_element_type=jnp.float32)
-
-    def entry(stream, at):
-        step, chunk = divmod(at, chunks)
-        leaves, sign = (has_up, -1) if stream == UP else (has_down, 1)
-        start, before_end = (0, line - 2) if stream == UP else (line - 1, 1)
-        if step == 0:
-            return col, chunk, (leaves,)
-        if step == line - 1:
-            if not balance or chunk + half >= chunks:
-                return None
-            return pair, chunk + half, (z == before_end,)
-        source = z + sign * step
-        inside = source >= 0 if stream == UP else source < line
-        if step == 1 and balance:
-            first = z == start
-            return jnp.where(first, pair, source * 2 + x), chunk, (leaves, jnp.logical_or(first, inside))
-        return source * 2 + x, chunk, (leaves, inside)
-
-    open_sends = []
-
-    def start(stream, block, chunk, *conds):
+        part[...] = total
+
+    sends = []
+
+    def send(stream, block, chunk, *conds):
         when(*conds)(lambda: move(stream, block, chunk).start())
-
-    def finish(stream, block, chunk, *conds):
-        when(*conds)(lambda: move(stream, block, chunk).wait_send())
-
-    def advance(stream, tick):
-        new = entry(stream, tick + window)
-        if new is None:
-            return
-        if tick >= 0:
-            old = entry(stream, tick)
-            finish(stream, old[0], old[1], *old[2])
-            open_sends.remove((stream, tick))
-        start(stream, new[0], new[1], *new[2])
-        open_sends.append((stream, tick + window))
-
-    across = []
-
-    def start_across(block, chunk, *conds):
-        start(ACROSS, block, chunk, *conds)
-        across.append((block, chunk, conds))
+        sends.append((stream, block, chunk, conds))
 
     def across_ok(of_z, chunk):
         if not balance:
             return ()
-        conds = [
-            jnp.logical_not(jnp.logical_and(z == 1, of_z == 0)),
-            jnp.logical_not(jnp.logical_and(z == line - 2, of_z == line - 1)),
-        ]
         if chunk >= half:
-            conds.append(jnp.logical_not(jnp.logical_and(z == 0, of_z == 1)))
-            conds.append(jnp.logical_not(jnp.logical_and(z == line - 1, of_z == line - 2)))
-        return conds
-
-    def pass_across(step, chunk):
+            return of_z != 0, of_z != line - 1
+        return (jnp.logical_not(jnp.logical_and(z == 1, of_z == 0)),
+                jnp.logical_not(jnp.logical_and(z == line - 2, of_z == line - 1)))
+
+    def take_pair(step):
+        for at, there in ((z - 1 - step, z - 1 - step >= 0), (z + 1 + step, z + 1 + step < line)):
+            block = at * 2 + other
+
+            @pl.when(there)
+            def _():
+                for chunk in range(chunks):
+                    if balance and chunk >= half:
+                        passed_on = jnp.logical_and(
+                            jnp.logical_or(at == 0, at == line - 1), jnp.logical_and(has_up, has_down))
+                        receive(block, chunk, jnp.logical_not(passed_on))
+                    else:
+                        receive(block, chunk)
+                multiply(block)
+
+    bottom, top = other, (line - 1) * 2 + other
+
+    for chunk in range(chunks):
+        send(UP, col, chunk, has_up)
+        send(DOWN, col, chunk, has_down)
+        send(ACROSS, col, chunk)
+    multiply(col)
+
+    for step in range(line - 1):
         below, above = z - 1 - step, z + 1 + step
-        start_across(below * 2 + x, chunk, below >= 0, *across_ok(below, chunk))
-        start_across(above * 2 + x, chunk, above < line, *across_ok(above, chunk))
-
-    def take(block, chunk, *conds):
-        receive(block, chunk, *conds)
-        multiply(block, chunk, *conds)
-
-    def take_pair(step, chunk):
-        below, above = z - 1 - step, z + 1 + step
-        late = balance and step == 0 and chunk >= half
-        take(below * 2 + other, chunk, below >= 0, z != line - 1 if late else True)
-        take(above * 2 + other, chunk, above < line, z != 0 if late else True)
-
-    for chunk in range(window):
-        advance(UP, chunk - window)
-        advance(DOWN, chunk - window)
-        start_across(col, chunk)
-    for chunk in range(chunks):
-        multiply(col, chunk)
-
-    for tick in range(ticks):
-        step, chunk = divmod(tick, chunks)
-        below, above = z - 1 - step, z + 1 + step
-        receive(below * 2 + x, chunk, below >= 0)
-        advance(UP, tick)
-        receive(above * 2 + x, chunk, above < line)
-        advance(DOWN, tick)
-        if tick + window < chunks:
-            start_across(col, tick + window)
-        if 0 <= tick - window < chunks:
-            pass_across(0, tick - window)
-        if step >= 1:
-            pass_across(step, chunk)
-        multiply(below * 2 + x, chunk, below >= 0)
-        multiply(above * 2 + x, chunk, above < line)
+        for chunk in range(chunks):
+            receive(below * 2 + x, chunk, below >= 0)
+            send(UP, below * 2 + x, chunk, below >= 0, has_up)
+            send(ACROSS, below * 2 + x, chunk, below >= 0, *across_ok(below, chunk))
+            receive(above * 2 + x, chunk, above < line)
+            send(DOWN, above * 2 + x, chunk, above < line, has_down)
+            send(ACROSS, above * 2 + x, chunk, above < line, *across_ok(above, chunk))
+        if balance and step >= 1:
+            for chunk in range(half, chunks):
+                receive(bottom, chunk, z == step)
+                send(UP, bottom, chunk, z == step)
+                receive(top, chunk, z == line - 1 - step)
+                send(DOWN, top, chunk, z == line - 1 - step)
+        pl.when(below >= 0)(lambda: multiply(below * 2 + x))
+        pl.when(above < line)(lambda: multiply(above * 2 + x))
         if step == 0:
-            take(pair, chunk)
-        if step >= 2:
-            take_pair(step - 2, chunk)
-    for tick in range(ticks, ticks + chunks - half - window):
-        advance(UP, tick)
-        advance(DOWN, tick)
-    for step in range(max(line - 3, 0), line - 1):
-        for chunk in range(chunks):
-            take_pair(step, chunk)
-            if step == line - 2 and balance and chunk >= half:
-                take(2 + other, chunk, z == 0)
-                take((line - 2) * 2 + other, chunk, z == line - 1)
+            for chunk in range(chunks):
+                receive(pair, chunk)
+                if balance:
+                    send(UP, pair, chunk, z == 0)
+                    send(DOWN, pair, chunk, z == line - 1)
+            multiply(pair)
+        else:
+            take_pair(step - 1)
+    take_pair(line - 2)
 
     def sum_copy(piece, source):
         return pltpu.make_async_remote_copy(
@@ -249,11 +207,8 @@
             mine = jnp.logical_and(row == piece, col == factor * row + at)
             pl.when(jnp.logical_not(mine))(lambda: low_copy(piece, at, row, col).wait_recv())
 
-    for stream, at in open_sends:
-        block, chunk, conds = entry(stream, at)
-        finish(stream, block, chunk, *conds)
-    for block, chunk, conds in across:
-        finish(ACROSS, block, chunk, *conds)
+    for stream, block, chunk, conds in sends:
+        when(*conds)(lambda: move(stream, block, chunk).wait_send())
     for piece in range(pieces):
         pl.when(row != piece)(lambda: sum_copy(piece, row).wait_send())
 
@@ -324,7 +279,7 @@
         cost_estimate=pl.CostEstimate(
             flops=2 * columns * n_states * width, bytes_accessed=2 * n_states * width, transcendentals=0),
         name="pull",
-    )(inverse_slab, cot_solved)
+    )(inverse_slab, pltpu.with_memory_space_constraint(cot_solved, pltpu.HBM))
 
     panel_width = solved_panel.shape[1]
     tile = min(panel_width, 512)

time: 43.3 us -> 38.6 us (0.89)
  Pallas kernels: 41.5 us -> 37.8 us
  local copies, waits for them, and re-layouts: 0.95 us -> 0.01 us
    pallas_call x1, Pallas kernels: 37.7 us -> 34 us  [body(): pl.pallas_call(functools.partial(pull_kernel, n_row, n_col, pieces, chunk...]
    unnamed x6 -> x4, local copies, waits for them, and re-layouts: 0.95 us -> 0.01 us
where the time goes in v3:
time: 38.6 us; the launch traced here: 38.5 us
  Pallas kernels  37.8 us (98%)
  between operations  0.67 us (2%)
    pallas_call x1, Pallas kernels, body(): pl.pallas_call(functools.partial(pull_kernel, n_row, n_col, pieces, chunk...  34 us
    pallas_call x1, Pallas kernels, body(): pl.pallas_call(functools.partial(operator_kernel, tile), out_shape=(jax.S...  3.78 us

profile of v3, /device:TPU:0, one launch (start us, length us, event | category | flops | bytes accessed | tf_op | source)
XLA Modules:
  0.0 38.5 jit_solution(886242083343150786)
XLA Ops:
  0.6 0.0 copy-start
  0.6 0.0 copy-start.1
  0.7 34.0 %pull.1 = (bf16[2,64,256]{2,1,0:T(8,128)(2,1)S(1)}, f32[64,256]{1,0:T(8,128)S(1)}) custom-call(bf16[16384,256]{1,0:T(8,128)(2,1)} %inverse_ref.1, bf16[64,2048]{1,0:T(8,128)(2,1)} %cot_ref.1), custom_call_target="tpu_custom_call" | custom-call | flops 536870912 | bytes 8388608 | tf_op jit(solution)/shard_map/pull/pallas_call | solution.py:259
  34.7 0.0 copy-done
  34.7 0.0 copy-done.1
  34.7 3.8 %operator.1 = (f32[64,256]{1,0:T(8,128)}, bf16[512,8192]{1,0:T(8,128)(2,1)}) custom-call(bf16[2,64,256]{2,1,0:T(8,128)(2,1)S(1)} %get-tuple-element.4.needed_ref, bf16[64,8192]{1,0:T(8,128)(2,1)S(1)} %copy-done, bf16[64,256]{1,0:T(8,128)(2,1)S(1)} %copy-done.1, f32[64,256]{1,0:T(8,128)S(1)} %get-tuple-element.5.pulled_ref), custom_call_target="tpu_custom_call" | custom-call | flops 536870912 | bytes 8388608 | tf_op jit(solution)/shard_map/operator/pallas_call | solution.py:287
Async XLA Ops:
  0.6 34.1 %copy-start = (bf16[64,8192]{1,0:T(8,128)(2,1)S(1)}, bf16[64,8192]{1,0:T(8,128)(2,1)}, u32[]{:S(2)}) copy-start(bf16[64,8192]{1,0:T(8,128)(2,1)} %panel_ref.1) | copy-start | bytes 3145732
  0.6 34.1 %copy-start.1 = (bf16[64,256]{1,0:T(8,128)(2,1)S(1)}, bf16[64,256]{1,0:T(8,128)(2,1)}, u32[]{:S(2)}) copy-start(bf16[64,256]{1,0:T(8,128)(2,1)} %direct_ref.1) | copy-start | bytes 98308

commit v4 on v3

--- a/solution.py
+++ b/solution.py
@@ -60,8 +60,7 @@
     for step in range(1, n_row):
         greet(lax.rem(row + step, n_row), col)
 
-    for at in range(n_col):
-        load_inverse(lax.rem(col + at, n_col)).start()
+    load_inverse(col).start()
     part[...] = jnp.zeros_like(part)
     for chunk in range(chunks):
         load_own(chunk).wait()
@@ -80,10 +79,11 @@
     def receive(block, chunk, *conds):
         when(*conds)(lambda: move(ACROSS, block, chunk).wait_recv())
 
-    def multiply(block):
-        load_inverse(block).wait()
+    def multiply(block, which=tuple(range(chunks))):
+        if which[0] == 0:
+            load_inverse(block).wait()
         total = part[...]
-        for chunk in range(chunks):
+        for chunk in which:
             span = pl.ds(pl.multiple_of(block * depth + chunk * span_of, span_of), span_of)
             total += jnp.dot(
                 gathered[block, chunk], inverse[span, :], preferred_element_type=jnp.float32)
@@ -124,10 +124,20 @@
         send(UP, col, chunk, has_up)
         send(DOWN, col, chunk, has_down)
         send(ACROSS, col, chunk)
+
+    def load_step(step):
+        for at, there in ((z - 1 - step, z - 1 - step >= 0), (z + 1 + step, z + 1 + step < line)):
+            for side in (x, other):
+                pl.when(there)(lambda: load_inverse(at * 2 + side).start())
+
+    load_inverse(pair).start()
+    load_step(0)
     multiply(col)
 
     for step in range(line - 1):
         below, above = z - 1 - step, z + 1 + step
+        if step >= 1:
+            load_step(step)
         for chunk in range(chunks):
             receive(below * 2 + x, chunk, below >= 0)
             send(UP, below * 2 + x, chunk, below >= 0, has_up)
@@ -152,7 +162,15 @@
             multiply(pair)
         else:
             take_pair(step - 1)
-    take_pair(line - 2)
+    order = [chunk for both in zip(range(half), range(half, chunks)) for chunk in both] if balance else []
+    for at, there in ((0, jnp.logical_not(has_up)), (line - 1, jnp.logical_not(has_down))):
+        block = at * 2 + other
+
+        @pl.when(there)
+        def _():
+            for chunk in order or range(chunks):
+                receive(block, chunk)
+                multiply(block, (chunk,))
 
     def sum_copy(piece, source):
         return pltpu.make_async_remote_copy(
@@ -201,12 +219,6 @@
         def _():
             needed_ref[slot, span, :] = low[...]
 
-    for piece in range(pieces):
-        pl.when(row != piece)(lambda: total_copy(piece, row).wait_recv())
-        for at in range(factor):
-            mine = jnp.logical_and(row == piece, col == factor * row + at)
-            pl.when(jnp.logical_not(mine))(lambda: low_copy(piece, at, row, col).wait_recv())
-
     for stream, block, chunk, conds in sends:
         when(*conds)(lambda: move(stream, block, chunk).wait_send())
     for piece in range(pieces):
@@ -219,6 +231,12 @@
             pl.when(jnp.logical_not(mine))(lambda: low_copy(row, slot, user, to_col).wait_send())
         for step in range(1, n_row):
             total_copy(row, lax.rem(row + step, n_row)).wait_send()
+
+    for piece in range(pieces):
+        pl.when(row != piece)(lambda: total_copy(piece, row).wait_recv())
+        for at in range(factor):
+            mine = jnp.logical_and(row == piece, col == factor * row + at)
+            pl.when(jnp.logical_not(mine))(lambda: low_copy(piece, at, row, col).wait_recv())
 
 
 def operator_kernel(tile, needed_ref, panel_ref, direct_ref, pulled_ref, factor_ref, operator_ref,

time: 38.6 us -> 38.4 us (level)
  no operation moved by 1% of the time
where the time goes in v4:
time: 38.4 us; the launch traced here: 38.2 us
  Pallas kernels  37.6 us (98%)
  between operations  0.67 us (2%)
    pallas_call x1, Pallas kernels, body(): pl.pallas_call(functools.partial(pull_kernel, n_row, n_col, pieces, chunk...  33.8 us
    pallas_call x1, Pallas kernels, body(): pl.pallas_call(functools.partial(operator_kernel, tile), out_shape=(jax.S...  3.78 us

profile of v4, /device:TPU:0, one launch (start us, length us, event | category | flops | bytes accessed | tf_op | source)
XLA Modules:
  0.0 38.2 jit_solution(3916043747646116880)
XLA Ops:
  0.6 0.0 copy-start
  0.6 0.0 copy-start.1
  0.7 33.8 %pull.1 = (bf16[2,64,256]{2,1,0:T(8,128)(2,1)S(1)}, f32[64,256]{1,0:T(8,128)S(1)}) custom-call(bf16[16384,256]{1,0:T(8,128)(2,1)} %inverse_ref.1, bf16[64,2048]{1,0:T(8,128)(2,1)} %cot_ref.1), custom_call_target="tpu_custom_call" | custom-call | flops 536870912 | bytes 8388608 | tf_op jit(solution)/shard_map/pull/pallas_call | solution.py:277
  34.4 0.0 copy-done
  34.5 0.0 copy-done.1
  34.5 3.8 %operator.1 = (f32[64,256]{1,0:T(8,128)}, bf16[512,8192]{1,0:T(8,128)(2,1)}) custom-call(bf16[2,64,256]{2,1,0:T(8,128)(2,1)S(1)} %get-tuple-element.4.needed_ref, bf16[64,8192]{1,0:T(8,128)(2,1)S(1)} %copy-done, bf16[64,256]{1,0:T(8,128)(2,1)S(1)} %copy-done.1, f32[64,256]{1,0:T(8,128)S(1)} %get-tuple-element.5.pulled_ref), custom_call_target="tpu_custom_call" | custom-call | flops 536870912 | bytes 8388608 | tf_op jit(solution)/shard_map/operator/pallas_call | solution.py:305
Async XLA Ops:
  0.6 33.8 %copy-start = (bf16[64,8192]{1,0:T(8,128)(2,1)S(1)}, bf16[64,8192]{1,0:T(8,128)(2,1)}, u32[]{:S(2)}) copy-start(bf16[64,8192]{1,0:T(8,128)(2,1)} %panel_ref.1) | copy-start | bytes 3145732
  0.6 33.8 %copy-start.1 = (bf16[64,256]{1,0:T(8,128)(2,1)S(1)}, bf16[64,256]{1,0:T(8,128)(2,1)}, u32[]{:S(2)}) copy-start(bf16[64,256]{1,0:T(8,128)(2,1)} %direct_ref.1) | copy-start | bytes 98308

commit v5 on v4

--- a/solution.py
+++ b/solution.py
@@ -270,7 +270,7 @@
     columns, depth = cot_solved.shape
     factor = n_col // n_row
     pieces = min(n_row, columns // PIECE)
-    chunks = 4 if depth >= 1024 else 1
+    chunks = 2 if depth >= 1024 else 1
     hbm = pl.BlockSpec(memory_space=pltpu.HBM)
     vmem = pl.BlockSpec(memory_space=pltpu.VMEM)
     dma = pltpu.SemaphoreType.DMA
@@ -300,7 +300,7 @@
     )(inverse_slab, pltpu.with_memory_space_constraint(cot_solved, pltpu.HBM))
 
     panel_width = solved_panel.shape[1]
-    tile = min(panel_width, 512)
+    tile = min(panel_width, 1024)
     tiles = panel_width // tile
     return pl.pallas_call(
         functools.partial(operator_kernel, tile),

time: 38.4 us -> 39.4 us (1.026)
  Pallas kernels: 37.6 us -> 38.5 us
    pallas_call x1, Pallas kernels: 33.8 us -> 34.7 us  [body(): pl.pallas_call(functools.partial(pull_kernel, n_row, n_col, pieces, chunk...]
where the time goes in v5:
time: 39.4 us; the launch traced here: 39.2 us
  Pallas kernels  38.5 us (98%)
  between operations  0.67 us (2%)
    pallas_call x1, Pallas kernels, body(): pl.pallas_call(functools.partial(pull_kernel, n_row, n_col, pieces, chunk...  34.7 us
    pallas_call x1, Pallas kernels, body(): pl.pallas_call(functools.partial(operator_kernel, tile), out_shape=(jax.S...  3.87 us

profile of v5, /device:TPU:0, one launch (start us, length us, event | category | flops | bytes accessed | tf_op | source)
XLA Modules:
  0.0 39.2 jit_solution(10200508277735230370)
XLA Ops:
  0.6 0.0 copy-start
  0.6 0.0 copy-start.1
  0.7 34.7 %pull.1 = (bf16[2,64,256]{2,1,0:T(8,128)(2,1)S(1)}, f32[64,256]{1,0:T(8,128)S(1)}) custom-call(bf16[16384,256]{1,0:T(8,128)(2,1)} %inverse_ref.1, bf16[64,2048]{1,0:T(8,128)(2,1)} %cot_ref.1), custom_call_target="tpu_custom_call" | custom-call | flops 536870912 | bytes 8388608 | tf_op jit(solution)/shard_map/pull/pallas_call | solution.py:277
  35.3 0.0 copy-done
  35.3 0.0 copy-done.1
  35.4 3.9 %operator.1 = (f32[64,256]{1,0:T(8,128)}, bf16[512,8192]{1,0:T(8,128)(2,1)}) custom-call(bf16[2,64,256]{2,1,0:T(8,128)(2,1)S(1)} %get-tuple-element.4.needed_ref, bf16[64,8192]{1,0:T(8,128)(2,1)S(1)} %copy-done, bf16[64,256]{1,0:T(8,128)(2,1)S(1)} %copy-done.1, f32[64,256]{1,0:T(8,128)S(1)} %get-tuple-element.5.pulled_ref), custom_call_target="tpu_custom_call" | custom-call | flops 536870912 | bytes 8388608 | tf_op jit(solution)/shard_map/operator/pallas_call | solution.py:305
Async XLA Ops:
  0.6 34.7 %copy-start = (bf16[64,8192]{1,0:T(8,128)(2,1)S(1)}, bf16[64,8192]{1,0:T(8,128)(2,1)}, u32[]{:S(2)}) copy-start(bf16[64,8192]{1,0:T(8,128)(2,1)} %panel_ref.1) | copy-start | bytes 3145732
  0.6 34.7 %copy-start.1 = (bf16[64,256]{1,0:T(8,128)(2,1)S(1)}, bf16[64,256]{1,0:T(8,128)(2,1)}, u32[]{:S(2)}) copy-start(bf16[64,256]{1,0:T(8,128)(2,1)} %direct_ref.1) | copy-start | bytes 98308

commit v6 on v4

--- a/solution.py
+++ b/solution.py
@@ -120,10 +120,14 @@
 
     bottom, top = other, (line - 1) * 2 + other
 
-    for chunk in range(chunks):
+    def send_own(chunk):
         send(UP, col, chunk, has_up)
         send(DOWN, col, chunk, has_down)
         send(ACROSS, col, chunk)
+
+    window = max(half, 1)
+    for chunk in range(window):
+        send_own(chunk)
 
     def load_step(step):
         for at, there in ((z - 1 - step, z - 1 - step >= 0), (z + 1 + step, z + 1 + step < line)):
@@ -133,6 +137,11 @@
     load_inverse(pair).start()
     load_step(0)
     multiply(col)
+    for chunk in range(window, chunks):
+        for stream, conds in ((UP, (has_up,)), (DOWN, (has_down,))):
+            when(*conds)(lambda: move(stream, col, chunk - window).wait_send())
+            sends.remove((stream, col, chunk - window, conds))
+        send_own(chunk)
 
     for step in range(line - 1):
         below, above = z - 1 - step, z + 1 + step
@@ -300,7 +309,7 @@
     )(inverse_slab, pltpu.with_memory_space_constraint(cot_solved, pltpu.HBM))
 
     panel_width = solved_panel.shape[1]
-    tile = min(panel_width, 512)
+    tile = min(panel_width, 256)
     tiles = panel_width // tile
     return pl.pallas_call(
         functools.partial(operator_kernel, tile),

time: 38.4 us -> 38.5 us (level)
  no operation moved by 1% of the time
where the time goes in v6:
time: 38.5 us; the launch traced here: 38.4 us
  Pallas kernels  37.7 us (98%)
  between operations  0.67 us (2%)
    pallas_call x1, Pallas kernels, body(): pl.pallas_call(functools.partial(pull_kernel, n_row, n_col, pieces, chunk...  33.8 us
    pallas_call x1, Pallas kernels, body(): pl.pallas_call(functools.partial(operator_kernel, tile), out_shape=(jax.S...  3.9 us

profile of v6, /device:TPU:0, one launch (start us, length us, event | category | flops | bytes accessed | tf_op | source)
XLA Modules:
  0.0 38.4 jit_solution(10677635630687046624)
XLA Ops:
  0.6 0.0 copy-start
  0.6 0.0 copy-start.1
  0.7 33.8 %pull.1 = (bf16[2,64,256]{2,1,0:T(8,128)(2,1)S(1)}, f32[64,256]{1,0:T(8,128)S(1)}) custom-call(bf16[16384,256]{1,0:T(8,128)(2,1)} %inverse_ref.1, bf16[64,2048]{1,0:T(8,128)(2,1)} %cot_ref.1), custom_call_target="tpu_custom_call" | custom-call | flops 536870912 | bytes 8388608 | tf_op jit(solution)/shard_map/pull/pallas_call | solution.py:286
  34.4 0.0 copy-done
  34.5 0.0 copy-done.1
  34.5 3.9 %operator.1 = (f32[64,256]{1,0:T(8,128)}, bf16[512,8192]{1,0:T(8,128)(2,1)}) custom-call(bf16[2,64,256]{2,1,0:T(8,128)(2,1)S(1)} %get-tuple-element.4.needed_ref, bf16[64,8192]{1,0:T(8,128)(2,1)S(1)} %copy-done, bf16[64,256]{1,0:T(8,128)(2,1)S(1)} %copy-done.1, f32[64,256]{1,0:T(8,128)S(1)} %get-tuple-element.5.pulled_ref), custom_call_target="tpu_custom_call" | custom-call | flops 536870912 | bytes 8388608 | tf_op jit(solution)/shard_map/operator/pallas_call | solution.py:314
Async XLA Ops:
  0.6 33.8 %copy-start = (bf16[64,8192]{1,0:T(8,128)(2,1)S(1)}, bf16[64,8192]{1,0:T(8,128)(2,1)}, u32[]{:S(2)}) copy-start(bf16[64,8192]{1,0:T(8,128)(2,1)} %panel_ref.1) | copy-start | bytes 3145732
  0.6 33.8 %copy-start.1 = (bf16[64,256]{1,0:T(8,128)(2,1)S(1)}, bf16[64,256]{1,0:T(8,128)(2,1)}, u32[]{:S(2)}) copy-start(bf16[64,256]{1,0:T(8,128)(2,1)} %direct_ref.1) | copy-start | bytes 98308

commit v7 on v4

--- a/solution.py
+++ b/solution.py
@@ -35,7 +35,7 @@
     depth = cot_ref.shape[1]
     span_of = depth // chunks
     balance = line >= 4
-    half = chunks // 2
+    split = chunks
     has_down, has_up = z > 0, z < line - 1
 
     def load_inverse(block):
@@ -98,7 +98,7 @@
     def across_ok(of_z, chunk):
         if not balance:
             return ()
-        if chunk >= half:
+        if chunk >= split:
             return of_z != 0, of_z != line - 1
         return (jnp.logical_not(jnp.logical_and(z == 1, of_z == 0)),
                 jnp.logical_not(jnp.logical_and(z == line - 2, of_z == line - 1)))
@@ -110,7 +110,7 @@
             @pl.when(there)
             def _():
                 for chunk in range(chunks):
-                    if balance and chunk >= half:
+                    if balance and chunk >= split:
                         passed_on = jnp.logical_and(
                             jnp.logical_or(at == 0, at == line - 1), jnp.logical_and(has_up, has_down))
                         receive(block, chunk, jnp.logical_not(passed_on))
@@ -120,10 +120,13 @@
 
     bottom, top = other, (line - 1) * 2 + other
 
-    for chunk in range(chunks):
+    def send_own(chunk):
         send(UP, col, chunk, has_up)
         send(DOWN, col, chunk, has_down)
         send(ACROSS, col, chunk)
+
+    for chunk in range(chunks):
+        send_own(chunk)
 
     def load_step(step):
         for at, there in ((z - 1 - step, z - 1 - step >= 0), (z + 1 + step, z + 1 + step < line)):
@@ -146,7 +149,7 @@
             send(DOWN, above * 2 + x, chunk, above < line, has_down)
             send(ACROSS, above * 2 + x, chunk, above < line, *across_ok(above, chunk))
         if balance and step >= 1:
-            for chunk in range(half, chunks):
+            for chunk in range(split, chunks):
                 receive(bottom, chunk, z == step)
                 send(UP, bottom, chunk, z == step)
                 receive(top, chunk, z == line - 1 - step)
@@ -162,13 +165,12 @@
             multiply(pair)
         else:
             take_pair(step - 1)
-    order = [chunk for both in zip(range(half), range(half, chunks)) for chunk in both] if balance else []
     for at, there in ((0, jnp.logical_not(has_up)), (line - 1, jnp.logical_not(has_down))):
         block = at * 2 + other
 
         @pl.when(there)
         def _():
-            for chunk in order or range(chunks):
+            for chunk in range(chunks):
                 receive(block, chunk)
                 multiply(block, (chunk,))
 

time: 38.4 us -> 40.9 us (1.065)
  the two profiles are of different devices: /device:TPU:0 before, /device:TPU:7 now
where the time goes in v7:
time: 40.9 us; the launch traced here: 40.7 us
  Pallas kernels  40.1 us (98%)
  between operations  0.67 us (2%)
    pallas_call x1, Pallas kernels, body(): pl.pallas_call(functools.partial(pull_kernel, n_row, n_col, pieces, chunk...  36.3 us
    pallas_call x1, Pallas kernels, body(): pl.pallas_call(functools.partial(operator_kernel, tile), out_shape=(jax.S...  3.78 us

profile of v7, /device:TPU:7, one launch (start us, length us, event | category | flops | bytes accessed | tf_op | source)
XLA Modules:
  0.0 40.7 jit_solution(9416472652839568517)
XLA Ops:
  0.6 0.0 copy-start
  0.6 0.0 copy-start.1
  0.7 36.3 %pull.1 = (bf16[2,64,256]{2,1,0:T(8,128)(2,1)S(1)}, f32[64,256]{1,0:T(8,128)S(1)}) custom-call(bf16[16384,256]{1,0:T(8,128)(2,1)} %inverse_ref.1, bf16[64,2048]{1,0:T(8,128)(2,1)} %cot_ref.1), custom_call_target="tpu_custom_call" | custom-call | flops 536870912 | bytes 8388608 | tf_op jit(solution)/shard_map/pull/pallas_call | solution.py:279
  36.9 0.0 copy-done
  36.9 0.0 copy-done.1
  37.0 3.8 %operator.1 = (f32[64,256]{1,0:T(8,128)}, bf16[512,8192]{1,0:T(8,128)(2,1)}) custom-call(bf16[2,64,256]{2,1,0:T(8,128)(2,1)S(1)} %get-tuple-element.4.needed_ref, bf16[64,8192]{1,0:T(8,128)(2,1)S(1)} %copy-done, bf16[64,256]{1,0:T(8,128)(2,1)S(1)} %copy-done.1, f32[64,256]{1,0:T(8,128)S(1)} %get-tuple-element.5.pulled_ref), custom_call_target="tpu_custom_call" | custom-call | flops 536870912 | bytes 8388608 | tf_op jit(solution)/shard_map/operator/pallas_call | solution.py:307
Async XLA Ops:
  0.6 36.3 %copy-start = (bf16[64,8192]{1,0:T(8,128)(2,1)S(1)}, bf16[64,8192]{1,0:T(8,128)(2,1)}, u32[]{:S(2)}) copy-start(bf16[64,8192]{1,0:T(8,128)(2,1)} %panel_ref.1) | copy-start | bytes 3145732
  0.6 36.3 %copy-start.1 = (bf16[64,256]{1,0:T(8,128)(2,1)S(1)}, bf16[64,256]{1,0:T(8,128)(2,1)}, u32[]{:S(2)}) copy-start(bf16[64,256]{1,0:T(8,128)(2,1)} %direct_ref.1) | copy-start | bytes 98308

commit v8 on v7

--- a/solution.py
+++ b/solution.py
@@ -35,7 +35,7 @@
     depth = cot_ref.shape[1]
     span_of = depth // chunks
     balance = line >= 4
-    split = chunks
+    split = max(1, chunks // 4)
     has_down, has_up = z > 0, z < line - 1
 
     def load_inverse(block):
@@ -154,17 +154,21 @@
                 send(UP, bottom, chunk, z == step)
                 receive(top, chunk, z == line - 1 - step)
                 send(DOWN, top, chunk, z == line - 1 - step)
-        pl.when(below >= 0)(lambda: multiply(below * 2 + x))
-        pl.when(above < line)(lambda: multiply(above * 2 + x))
         if step == 0:
             for chunk in range(chunks):
                 receive(pair, chunk)
                 if balance:
                     send(UP, pair, chunk, z == 0)
                     send(DOWN, pair, chunk, z == line - 1)
+        pl.when(below >= 0)(lambda: multiply(below * 2 + x))
+        pl.when(above < line)(lambda: multiply(above * 2 + x))
+        if step == 0:
             multiply(pair)
-        else:
-            take_pair(step - 1)
+        if step >= 2:
+            take_pair(step - 2)
+    if line >= 3:
+        take_pair(line - 3)
+
     for at, there in ((0, jnp.logical_not(has_up)), (line - 1, jnp.logical_not(has_down))):
         block = at * 2 + other
 

time: 40.9 us -> 39.4 us (0.963)
  the two profiles are of different devices: /device:TPU:7 before, /device:TPU:0 now
where the time goes in v8:
time: 39.4 us; the launch traced here: 39.2 us
  Pallas kernels  38.5 us (98%)
  between operations  0.67 us (2%)
    pallas_call x1, Pallas kernels, body(): pl.pallas_call(functools.partial(pull_kernel, n_row, n_col, pieces, chunk...  34.8 us
    pallas_call x1, Pallas kernels, body(): pl.pallas_call(functools.partial(operator_kernel, tile), out_shape=(jax.S...  3.78 us

profile of v8, /device:TPU:0, one launch (start us, length us, event | category | flops | bytes accessed | tf_op | source)
XLA Modules:
  0.0 39.2 jit_solution(9611208245031989453)
XLA Ops:
  0.6 0.0 copy-start
  0.6 0.0 copy-start.1
  0.7 34.8 %pull.1 = (bf16[2,64,256]{2,1,0:T(8,128)(2,1)S(1)}, f32[64,256]{1,0:T(8,128)S(1)}) custom-call(bf16[16384,256]{1,0:T(8,128)(2,1)} %inverse_ref.1, bf16[64,2048]{1,0:T(8,128)(2,1)} %cot_ref.1), custom_call_target="tpu_custom_call" | custom-call | flops 536870912 | bytes 8388608 | tf_op jit(solution)/shard_map/pull/pallas_call | solution.py:283
  35.4 0.0 copy-done
  35.4 0.0 copy-done.1
  35.4 3.8 %operator.1 = (f32[64,256]{1,0:T(8,128)}, bf16[512,8192]{1,0:T(8,128)(2,1)}) custom-call(bf16[2,64,256]{2,1,0:T(8,128)(2,1)S(1)} %get-tuple-element.4.needed_ref, bf16[64,8192]{1,0:T(8,128)(2,1)S(1)} %copy-done, bf16[64,256]{1,0:T(8,128)(2,1)S(1)} %copy-done.1, f32[64,256]{1,0:T(8,128)S(1)} %get-tuple-element.5.pulled_ref), custom_call_target="tpu_custom_call" | custom-call | flops 536870912 | bytes 8388608 | tf_op jit(solution)/shard_map/operator/pallas_call | solution.py:311
Async XLA Ops:
  0.6 34.8 %copy-start = (bf16[64,8192]{1,0:T(8,128)(2,1)S(1)}, bf16[64,8192]{1,0:T(8,128)(2,1)}, u32[]{:S(2)}) copy-start(bf16[64,8192]{1,0:T(8,128)(2,1)} %panel_ref.1) | copy-start | bytes 3145732
  0.6 34.8 %copy-start.1 = (bf16[64,256]{1,0:T(8,128)(2,1)S(1)}, bf16[64,256]{1,0:T(8,128)(2,1)}, u32[]{:S(2)}) copy-start(bf16[64,256]{1,0:T(8,128)(2,1)} %direct_ref.1) | copy-start | bytes 98308

commit v9 on v8

--- a/solution.py
+++ b/solution.py
@@ -35,7 +35,7 @@
     depth = cot_ref.shape[1]
     span_of = depth // chunks
     balance = line >= 4
-    split = max(1, chunks // 4)
+    split = max(1, chunks // 2)
     has_down, has_up = z > 0, z < line - 1
 
     def load_inverse(block):
@@ -164,19 +164,20 @@
         pl.when(above < line)(lambda: multiply(above * 2 + x))
         if step == 0:
             multiply(pair)
-        if step >= 2:
-            take_pair(step - 2)
-    if line >= 3:
-        take_pair(line - 3)
+        if step >= 1:
+            take_pair(step - 1)
 
     for at, there in ((0, jnp.logical_not(has_up)), (line - 1, jnp.logical_not(has_down))):
         block = at * 2 + other
 
         @pl.when(there)
         def _():
-            for chunk in range(chunks):
-                receive(block, chunk)
-                multiply(block, (chunk,))
+            group = max(1, chunks // 4)
+            for first in range(0, chunks, group):
+                some = tuple(range(first, first + group))
+                for chunk in some:
+                    receive(block, chunk)
+                multiply(block, some)
 
     def sum_copy(piece, source):
         return pltpu.make_async_remote_copy(
@@ -276,7 +277,7 @@
     columns, depth = cot_solved.shape
     factor = n_col // n_row
     pieces = min(n_row, columns // PIECE)
-    chunks = 4 if depth >= 1024 else 1
+    chunks = 8 if depth >= 1024 else 1
     hbm = pl.BlockSpec(memory_space=pltpu.HBM)
     vmem = pl.BlockSpec(memory_space=pltpu.VMEM)
     dma = pltpu.SemaphoreType.DMA

time: 39.4 us -> 39.3 us (level)
  no operation moved by 1% of the time
where the time goes in v9:
time: 39.3 us; the launch traced here: 39 us
  Pallas kernels  38.3 us (97%)
  between operations  0.67 us (2%)
    pallas_call x1, Pallas kernels, body(): pl.pallas_call(functools.partial(pull_kernel, n_row, n_col, pieces, chunk...  34.6 us
    pallas_call x1, Pallas kernels, body(): pl.pallas_call(functools.partial(operator_kernel, tile), out_shape=(jax.S...  3.78 us

profile of v9, /device:TPU:0, one launch (start us, length us, event | category | flops | bytes accessed | tf_op | source)
XLA Modules:
  0.0 39.0 jit_solution(2843279001598375700)
XLA Ops:
  0.6 0.0 copy-start
  0.6 0.0 copy-start.1
  0.7 34.6 %pull.1 = (bf16[2,64,256]{2,1,0:T(8,128)(2,1)S(1)}, f32[64,256]{1,0:T(8,128)S(1)}) custom-call(bf16[16384,256]{1,0:T(8,128)(2,1)} %inverse_ref.1, bf16[64,2048]{1,0:T(8,128)(2,1)} %cot_ref.1), custom_call_target="tpu_custom_call" | custom-call | flops 536870912 | bytes 8388608 | tf_op jit(solution)/shard_map/pull/pallas_call | solution.py:284
  35.2 0.0 copy-done
  35.2 0.0 copy-done.1
  35.2 3.8 %operator.1 = (f32[64,256]{1,0:T(8,128)}, bf16[512,8192]{1,0:T(8,128)(2,1)}) custom-call(bf16[2,64,256]{2,1,0:T(8,128)(2,1)S(1)} %get-tuple-element.4.needed_ref, bf16[64,8192]{1,0:T(8,128)(2,1)S(1)} %copy-done, bf16[64,256]{1,0:T(8,128)(2,1)S(1)} %copy-done.1, f32[64,256]{1,0:T(8,128)S(1)} %get-tuple-element.5.pulled_ref), custom_call_target="tpu_custom_call" | custom-call | flops 536870912 | bytes 8388608 | tf_op jit(solution)/shard_map/operator/pallas_call | solution.py:312
Async XLA Ops:
  0.6 34.6 %copy-start = (bf16[64,8192]{1,0:T(8,128)(2,1)S(1)}, bf16[64,8192]{1,0:T(8,128)(2,1)}, u32[]{:S(2)}) copy-start(bf16[64,8192]{1,0:T(8,128)(2,1)} %panel_ref.1) | copy-start | bytes 3145732
  0.6 34.6 %copy-start.1 = (bf16[64,256]{1,0:T(8,128)(2,1)S(1)}, bf16[64,256]{1,0:T(8,128)(2,1)}, u32[]{:S(2)}) copy-start(bf16[64,256]{1,0:T(8,128)(2,1)} %direct_ref.1) | copy-start | bytes 98308
